TPU v7x, 256 devices: a whole 4x4x8 slice. The times are simulated.
256 devices in a mesh: seq: 8 (over y_hi, x), row: 8 (over z), col: 4 (over y_lo, core).
Axes of the slice: x: 4, y: 4 (y_hi: 2, y_lo: 2; y = y_hi * 2 + y_lo), z: 8, core: 2. Of those that a mesh axis runs over, the one named last changes fastest.
Arguments:
- alignment: int32 [32768, 256], P('seq'), may hold values from 0 to 20, as said below
- cluster_sizes: int32 [32768], P('seq'), may hold values from 1 to 32, as said below
- block_inverse: float32 [128, 128], replicated, may hold values from -12 to 12
Outputs:
- couplings: float32 [5120, 5120], P(('seq', 'row'), 'col')
Inputs may be any that keep to these rules, and one draw needn't show every extreme that they name: `alignment`: the value 20 marks a gap. `cluster_sizes`: every cluster size is a power of two.
All inputs are finite; a program needn't handle non-finite values.
Results may differ from a plain program's by a relative error of at most 0.0003.
Values sent between devices are 32-bit elements; how exact they have to be, the bound alone decides.
A program may use at most 64 MiB of HBM per device.

v0:
```python
import jax
import jax.numpy as jnp
from jax import lax
from jax.sharding import PartitionSpec as P

Q = 20
POS = 256
PANEL = 128
PSEUDOCOUNT = 0.5


def spread(value, axis, source):
    kept = jnp.where(lax.axis_index(axis) == source, value, 0).astype(value.dtype)
    return lax.psum(kept, axis)


def one_hot_states(states):
    levels = lax.broadcasted_iota(jnp.int32, (1, 1, Q), 2)
    matches = (states[:, :, None] == levels).astype(jnp.bfloat16)
    return matches.reshape(states.shape[0], states.shape[1] * Q)


def covariance_block(pair_block, row_margin, col_margin, weight_total, row_start, col_start):
    row_freq = (1.0 - PSEUDOCOUNT) * row_margin / weight_total + PSEUDOCOUNT / Q
    col_freq = (1.0 - PSEUDOCOUNT) * col_margin / weight_total + PSEUDOCOUNT / Q
    shape_rc = pair_block.shape
    row_ids = row_start + lax.broadcasted_iota(jnp.int32, shape_rc, 0)
    col_ids = col_start + lax.broadcasted_iota(jnp.int32, shape_rc, 1)
    same_pos = row_ids // Q == col_ids // Q
    prior = jnp.where(
        same_pos, jnp.where(row_ids == col_ids, PSEUDOCOUNT / Q, 0.0), PSEUDOCOUNT / (Q * Q)
    )
    joint = (1.0 - PSEUDOCOUNT) * pair_block / weight_total + prior
    return joint - row_freq[:, None] * col_freq[None, :]


def accumulate_pairs(row_states, column_sets, span_widths, seq_weight):
    local_seqs = row_states.shape[0]
    block_rows = min(local_seqs, 1024)
    count_blocks = local_seqs // block_rows
    row_width = row_states.shape[1] * Q

    def blocked(states):
        return states.reshape(count_blocks, block_rows, states.shape[1])

    def add_block(running, block_item):
        pair_totals, row_margin, column_margins = running
        row_block, weight_block, column_blocks = block_item
        row_hot = one_hot_states(row_block)
        weighted = row_hot * weight_block[:, None]
        new_pairs = []
        new_margins = []
        for pair_total, margin_total, states_block, span_width in zip(
            pair_totals, column_margins, column_blocks, span_widths
        ):
            column_hot = one_hot_states(states_block)
            new_pairs.append(
                pair_total
                + lax.dot_general(
                    weighted,
                    column_hot,
                    (((0,), (0,)), ((), ())),
                    preferred_element_type=jnp.float32,
                )
            )
            new_margins.append(
                margin_total + jnp.dot(weight_block, column_hot, preferred_element_type=jnp.float32)
            )
        row_margin = row_margin + jnp.dot(weight_block, row_hot, preferred_element_type=jnp.float32)
        return ((tuple(new_pairs), row_margin, tuple(new_margins)), None)

    initial = (
        tuple((jnp.zeros((row_width, span_width), jnp.float32) for span_width in span_widths)),
        jnp.zeros((row_width,), jnp.float32),
        tuple((jnp.zeros((span_width,), jnp.float32) for span_width in span_widths)),
    )
    block_items = (
        blocked(row_states),
        seq_weight.reshape(count_blocks, block_rows),
        tuple((blocked(states) for states in column_sets)),
    )
    result, unused = lax.scan(add_block, initial, block_items)
    return result


def shards(alignment, cluster_sizes, block_inverse):
    seq_count = lax.axis_size("seq")
    row_count = lax.axis_size("row")
    col_count = lax.axis_size("col")
    seq_index = lax.axis_index("seq")
    row_index = lax.axis_index("row")
    col_index = lax.axis_index("col")
    local_seqs = alignment.shape[0]
    row_positions = POS // (seq_count * row_count)
    col_positions = POS // col_count
    block_features = row_positions * Q
    col_features = col_positions * Q
    seq_weight = (1.0 / cluster_sizes.astype(jnp.float32)).astype(jnp.bfloat16)
    grouped = alignment.reshape(local_seqs, seq_count, row_count, row_positions)
    row_states = lax.dynamic_slice_in_dim(grouped, row_index, 1, 2).reshape(
        local_seqs, seq_count * row_positions
    )
    col_states = lax.dynamic_slice_in_dim(alignment, col_index * col_positions, col_positions, 1)
    weight_local = jnp.sum(seq_weight.astype(jnp.float32))
    row_start = (seq_index * row_count + row_index) * block_features
    col_start = col_index * col_features
    pair_totals, row_margin, column_margins = accumulate_pairs(
        row_states, (col_states,), (col_features,), seq_weight
    )
    weight_total, row_margin, col_margin = lax.psum(
        (weight_local, row_margin, column_margins[0]), "seq"
    )
    pair_tile = lax.psum_scatter(pair_totals[0], "seq", scatter_dimension=0, tiled=True)
    own_margin = lax.dynamic_slice_in_dim(row_margin, seq_index * block_features, block_features)
    cov_tile = covariance_block(
        pair_tile, own_margin, col_margin, weight_total, row_start, col_start
    )
    panel_rows = spread(cov_tile[:, :PANEL], "col", 0)
    sym_inverse = 0.5 * (block_inverse + block_inverse.T)
    left_factor = jnp.dot(panel_rows, sym_inverse, precision=lax.Precision.HIGHEST)
    whole_panel = lax.all_gather(panel_rows, ("seq", "row"), axis=0, tiled=True)
    panel_cols = lax.dynamic_slice_in_dim(whole_panel, col_start, col_features, 0)
    update = lax.dot_general(
        left_factor, panel_cols, (((1,), (1,)), ((), ())), precision=lax.Precision.HIGHEST
    )
    return -Q * (cov_tile - update)


def solution(mesh):
    in_specs = (P("seq", None), P("seq"), P())
    out_specs = P(("seq", "row"), "col")
    return jax.shard_map(shards, mesh=mesh, in_specs=in_specs, out_specs=out_specs, check_vma=False)
```

profile of v0, /device:TPU:6, one launch (start us, length us, event | category | flops | bytes accessed | tf_op | source)
XLA Modules:
  0.0 306.2 jit_solution(9124577262664192869)
XLA Ops:
  6.5 5.6 %copy.9 = s32[4096,256]{0,1:T(8,128)} copy(s32[4096,256]{1,0:T(8,128)} %param.5) | data formatting | bytes 8388608 | tf_op args[0]
  12.1 2.2 constant_dynamic-slice_fusion.4
  14.3 0.6 copy.12
  14.9 5.2 %reshape.159 = s32[4096,8,8,4]{0,3,2,1:T(4,128)} reshape(s32[4096,256]{0,1:T(8,128)} %copy.9) | data formatting | bytes 8388608 | tf_op jit(solution)/shard_map/reshape | solution.py:99
  20.1 1.1 constant_dynamic-slice_fusion.5
  21.2 1.2 reshape_reshape.3
  22.5 0.7 convert_reduce_fusion
  23.1 51.7 %while.15 = (s32[]{:T(128)}, f32[640,1280]{1,0:T(8,128)}, f32[640]{0:T(1024)S(1)}, f32[1280]{0:T(1024)S(1)}, s32[4,1024,32]{1,0,2:T(4,128)}, /*index=5*/bf16[4,1...) while((s32[]{:T(128)}, f32[640,1280]{1,0:T(8,128)}, f32[640]{0:T(1024)S(1)}, ...), condition=%wide.region_1.2_spmd.clone, body=%wide.region_0.0_spmd.clone.sunk | while | flops 1686572800 | bytes 30978228 | solution.py:82
  23.2 1.5 constant_dynamic-slice_fusion.7
  24.8 0.5 broadcast_select_fusion.2
  25.2 1.2 mul.117
  26.5 0.9 iota_compare_fusion.4
  27.4 0.7 eq.120
  28.2 5.0 %convolution_add_fusion.2 = f32[640,1280]{1,0:T(8,128)} fusion(bf16[1024,640]{0,1:T(8,128)(2,1)} %mul.117, pred[1024,1280]{0,1:T(32,128)(4,1)S(1)} %eq.120, f32[640,1280]{1,0:T(8,128)} %get-tuple-element.161, pred[]{:T(512)S(6)} %compare.3), kind=kOutput, calls=%fused_computation.1.clone.1 | convolution fusion | flops 1679360000 | bytes 9175041 | tf_op jit(solution)/shard_map/while/body/eval_jaxpr/dot_general | solution.py:59
  33.2 0.8 convolution_reduce_fusion.5
  34.0 0.4 iota_compare_fusion.5
  34.4 0.4 eq.121
  34.8 0.5 convolution_reduce_fusion.4
  35.3 0.0 copy-done.1
  35.4 1.5 constant_dynamic-slice_fusion.7
  36.9 0.5 broadcast_select_fusion.2
  37.4 1.2 mul.117
  38.7 0.9 iota_compare_fusion.4
  39.6 0.7 eq.120
  40.3 6.0 %convolution_add_fusion.2 = f32[640,1280]{1,0:T(8,128)} fusion(bf16[1024,640]{0,1:T(8,128)(2,1)} %mul.117, pred[1024,1280]{0,1:T(32,128)(4,1)S(1)} %eq.120, f32[640,1280]{1,0:T(8,128)} %get-tuple-element.161, pred[]{:T(512)S(6)} %compare.3), kind=kOutput, calls=%fused_computation.1.clone.1 | convolution fusion | flops 1679360000 | bytes 9175041 | tf_op jit(solution)/shard_map/while/body/eval_jaxpr/dot_general | solution.py:59
  46.4 0.8 convolution_reduce_fusion.5
  47.2 0.4 iota_compare_fusion.5
  47.6 0.4 eq.121
  48.0 0.5 convolution_reduce_fusion.4
  48.5 1.5 constant_dynamic-slice_fusion.7
  50.1 0.5 broadcast_select_fusion.2
  50.6 1.2 mul.117
  51.8 0.9 iota_compare_fusion.4
  52.8 0.7 eq.120
  53.5 6.0 %convolution_add_fusion.2 = f32[640,1280]{1,0:T(8,128)} fusion(bf16[1024,640]{0,1:T(8,128)(2,1)} %mul.117, pred[1024,1280]{0,1:T(32,128)(4,1)S(1)} %eq.120, f32[640,1280]{1,0:T(8,128)} %get-tuple-element.161, pred[]{:T(512)S(6)} %compare.3), kind=kOutput, calls=%fused_computation.1.clone.1 | convolution fusion | flops 1679360000 | bytes 9175041 | tf_op jit(solution)/shard_map/while/body/eval_jaxpr/dot_general | solution.py:59
  59.6 0.8 convolution_reduce_fusion.5
  60.4 0.4 iota_compare_fusion.5
  60.8 0.4 eq.121
  61.2 0.5 convolution_reduce_fusion.4
  61.7 0.0 copy-done.1
  61.7 1.5 constant_dynamic-slice_fusion.7
  63.3 0.5 broadcast_select_fusion.2
  63.8 1.2 mul.117
  65.0 0.9 iota_compare_fusion.4
  66.0 0.7 eq.120
  66.7 6.0 %convolution_add_fusion.2 = f32[640,1280]{1,0:T(8,128)} fusion(bf16[1024,640]{0,1:T(8,128)(2,1)} %mul.117, pred[1024,1280]{0,1:T(32,128)(4,1)S(1)} %eq.120, f32[640,1280]{1,0:T(8,128)} %get-tuple-element.161, pred[]{:T(512)S(6)} %compare.3), kind=kOutput, calls=%fused_computation.1.clone.1 | convolution fusion | flops 1679360000 | bytes 9175041 | tf_op jit(solution)/shard_map/while/body/eval_jaxpr/dot_general | solution.py:59
  72.8 0.8 convolution_reduce_fusion.5
  73.6 0.4 iota_compare_fusion.5
  74.0 0.4 eq.121
  74.4 0.5 convolution_reduce_fusion.4
  74.9 0.0 copy-start.2
  74.9 0.0 reduce-scatter.2.cloned.1.call-update
  74.9 0.0 all-gather.2.cloned.1.call-start
  75.0 36.3 %all-reduce = (f32[1280]{0:T(1024)S(1)}, f32[]{:T(128)}, f32[640]{0:T(1024)S(1)}) all-reduce(f32[1280]{0:T(1024)S(1)} %get-tuple-element.46, f32[]{:T(128)} %get-tuple-element.102, f32[640]{0:T(1024)S(1)} %get-tuple-element.45), channel_id=1, replica_groups=mesh['seq'=8,'row'=8,'col'=4] {'seq'}, use_global_device_ids=true, to_apply=%region_6.7 | all-reduce | flops 1921 | bytes 15368 | tf_op jit(solution)/shard_map/psum | solution.py:110
  111.3 0.7 divide_add_fusion.1
  112.1 0.7 divide_add_fusion
  112.7 51.2 %reduce-scatter.2.cloned.1.call-done = f32[80,1280]{1,0:T(8,128)} async-done(((f32[640,1280]{1,0:T(8,128)}), f32[80,1280]{1,0:T(8,128)}) %reduce-scatter.2.cloned.1.call-update) | async-done | bytes 409616 | tf_op jit(solution)/shard_map/reduce_scatter | solution.py:113
  163.9 1.8 multiply_subtract_fusion
  165.8 11.4 %psum.31 = f32[80,128]{1,0:T(8,128)} all-reduce(f32[80,128]{1,0:T(8,128)S(1)} %slice_select_fusion), channel_id=1, replica_groups=mesh['seq'=8,'row'=8,'col'=4] {'col'}, use_global_device_ids=true, to_apply=%region_7.8 | all-reduce | flops 10240 | bytes 81920 | tf_op jit(solution)/shard_map/psum | solution.py:14
  177.2 0.0 all-gather.2.cloned.1.call-update
  177.2 0.1 copy.13
  177.3 1.0 fusion.6
  178.3 118.5 %all-gather.2.cloned.1.call-done = f32[5120,128]{1,0:T(8,128)} async-done(((f32[80,128]{1,0:T(8,128)}), f32[5120,128]{1,0:T(8,128)}) %all-gather.2.cloned.1.call-update) | async-done | bytes 2621456 | tf_op jit(solution)/shard_map/all_gather | solution.py:121
  296.8 2.6 fusion.3
  (49 shorter events, 0.5 us)
Async XLA Ops:
  6.5 157.4 %reduce-scatter.2.cloned.1.call-start = ((), (), s32[]{:S(2)}) async-start(), calls=%async_computation.1 | async-start | bytes 3686400 | tf_op jit(solution)/shard_map/reduce_scatter | solution.py:113
  20.1 2.3 copy-start.3
  23.1 3.3 %copy-start = (s32[4,1024,64]{1,2,0:T(8,128)}, s32[4,1024,64]{1,2,0:T(8,128)S(1)}, u32[]{:S(2)}) copy-start(s32[4,1024,64]{1,2,0:T(8,128)S(1)} %get-tuple-element.175) | copy-start | bytes 3145732 | tf_op jit(solution)/shard_map/while
  33.2 2.1 copy-start.1
  35.3 3.3 %copy-start = (s32[4,1024,64]{1,2,0:T(8,128)}, s32[4,1024,64]{1,2,0:T(8,128)S(1)}, u32[]{:S(2)}) copy-start(s32[4,1024,64]{1,2,0:T(8,128)S(1)} %get-tuple-element.175) | copy-start | bytes 3145732 | tf_op jit(solution)/shard_map/while
  46.4 2.1 copy-start.1
  48.5 3.3 %copy-start = (s32[4,1024,64]{1,2,0:T(8,128)}, s32[4,1024,64]{1,2,0:T(8,128)S(1)}, u32[]{:S(2)}) copy-start(s32[4,1024,64]{1,2,0:T(8,128)S(1)} %get-tuple-element.175) | copy-start | bytes 3145732 | tf_op jit(solution)/shard_map/while
  59.6 2.1 copy-start.1
  61.7 3.3 %copy-start = (s32[4,1024,64]{1,2,0:T(8,128)}, s32[4,1024,64]{1,2,0:T(8,128)S(1)}, u32[]{:S(2)}) copy-start(s32[4,1024,64]{1,2,0:T(8,128)S(1)} %get-tuple-element.175) | copy-start | bytes 3145732 | tf_op jit(solution)/shard_map/while
  72.8 2.1 copy-start.1
  74.9 102.3 %copy-start.2 = (f32[128,128]{1,0:T(8,128)S(1)}, f32[128,128]{1,0:T(8,128)}, u32[]{:S(2)}) copy-start(f32[128,128]{1,0:T(8,128)} %param.7) | copy-start | bytes 196612
  74.9 221.8 %all-gather.2.cloned.1.call-start = ((), (), s32[]{:S(2)}) async-start(), calls=%async_computation.2 | async-start | bytes 2662400 | tf_op jit(solution)/shard_map/all_gather | solution.py:121
Sparse Core Ops, SparseCore 0:
  75.0 88.8 reduce-scatter.1
  177.3 119.4 all-gather.1
where the time goes:
time: 307 us; the launch traced here: 306 us
  waiting for transfers between devices  170 us (55%)
  blocking collectives  47.6 us (16%)
  matrix products  31.8 us (10%)
  local copies, waits for them, and re-layouts  31.7 us (10%)
  between operations  13.5 us (4%)
  other arithmetic  11.4 us (4%)
    all_gather x1, waiting for transfers between devices, shards(): whole_panel = lax.all_gather(panel_rows, ('seq', 'row'), axis=0, tiled=True)  118 us
    reduce_scatter x1, waiting for transfers between devices, shards(): lax.psum_scatter(pair_totals[0], 'seq', scatter_dimension=0, tiled=True)  51.2 us
    psum x1, blocking collectives, shards(): lax.psum((weight_local, row_margin, column_margins[0]), 'seq')  36.3 us
    dot_general x4, matrix products, add_block(): lax.dot_general(weighted, column_hot, (((0,), (0,)), ((), ())), preferred...  23.1 us
    psum x1, blocking collectives, spread(): return lax.psum(kept, axis)  11.4 us
    dynamic_slice x12, local copies, waits for them, and re-layouts, accumulate_pairs(): result, unused = lax.scan(add_block, initial, block_items)  6.38 us
    unnamed x7, local copies, waits for them, and re-layouts  6.29 us
  transfers between devices with their start and end apart: 2, of which 2 were waited for; matrix products, arithmetic and copies ran while one was open for 1% of the time, Pallas kernels for 0%

commit v1 on v0

--- a/solution.py
+++ b/solution.py
@@ -11,7 +11,7 @@
 
 def spread(value, axis, source):
     kept = jnp.where(lax.axis_index(axis) == source, value, 0).astype(value.dtype)
-    return lax.psum(kept, axis)
+    return jnp.sum(lax.all_gather(kept, axis), axis=0)
 
 
 def one_hot_states(states):

time: 307 us -> 302 us (0.984)
  blocking collectives: 47.6 us -> 41.8 us
    psum x1 -> x0, blocking collectives: 11.4 us -> none  [spread(): return lax.psum(kept, axis)]
    all_gather x0 -> x1, blocking collectives: none -> 5.52 us  [spread(): return jnp.sum(lax.all_gather(kept, axis), axis=0)]
where the time goes in v1:
time: 302 us; the launch traced here: 301 us
  waiting for transfers between devices  170 us (56%)
  blocking collectives  41.8 us (14%)
  matrix products  31.8 us (11%)
  local copies, waits for them, and re-layouts  31.7 us (10%)
  between operations  13.5 us (4%)
  other arithmetic  12 us (4%)
    all_gather x1, waiting for transfers between devices, shards(): whole_panel = lax.all_gather(panel_rows, ('seq', 'row'), axis=0, tiled=True)  119 us
    reduce_scatter x1, waiting for transfers between devices, shards(): lax.psum_scatter(pair_totals[0], 'seq', scatter_dimension=0, tiled=True)  51.2 us
    psum x1, blocking collectives, shards(): lax.psum((weight_local, row_margin, column_margins[0]), 'seq')  36.3 us
    dot_general x4, matrix products, add_block(): lax.dot_general(weighted, column_hot, (((0,), (0,)), ((), ())), preferred...  23.1 us
    dynamic_slice x12, local copies, waits for them, and re-layouts, accumulate_pairs(): result, unused = lax.scan(add_block, initial, block_items)  6.38 us
    unnamed x7, local copies, waits for them, and re-layouts  6.29 us
  transfers between devices with their start and end apart: 2, of which 2 were waited for; matrix products, arithmetic and copies ran while one was open for 1% of the time, Pallas kernels for 0%

profile of v1, /device:TPU:6, one launch (start us, length us, event | category | flops | bytes accessed | tf_op | source)
XLA Modules:
  0.0 301.3 jit_solution(3417993990340295673)
XLA Ops:
  6.5 5.6 %copy.9 = s32[4096,256]{0,1:T(8,128)} copy(s32[4096,256]{1,0:T(8,128)} %param.5) | data formatting | bytes 8388608 | tf_op args[0]
  12.1 2.2 constant_dynamic-slice_fusion.4
  14.3 0.6 copy.12
  14.9 5.2 %reshape.159 = s32[4096,8,8,4]{0,3,2,1:T(4,128)} reshape(s32[4096,256]{0,1:T(8,128)} %copy.9) | data formatting | bytes 8388608 | tf_op jit(solution)/shard_map/reshape | solution.py:99
  20.1 1.1 constant_dynamic-slice_fusion.5
  21.2 1.2 reshape_reshape.3
  22.5 0.7 convert_reduce_fusion
  23.1 51.7 %while.15 = (s32[]{:T(128)}, f32[640,1280]{1,0:T(8,128)}, f32[640]{0:T(1024)S(1)}, f32[1280]{0:T(1024)S(1)}, s32[4,1024,32]{1,0,2:T(4,128)}, /*index=5*/bf16[4,1...) while((s32[]{:T(128)}, f32[640,1280]{1,0:T(8,128)}, f32[640]{0:T(1024)S(1)}, ...), condition=%wide.region_1.2_spmd.clone, body=%wide.region_0.0_spmd.clone.sunk | while | flops 1686572800 | bytes 30978228 | solution.py:82
  23.2 1.5 constant_dynamic-slice_fusion.7
  24.8 0.5 broadcast_select_fusion.2
  25.2 1.2 mul.117
  26.5 0.9 iota_compare_fusion.4
  27.4 0.7 eq.120
  28.2 5.0 %convolution_add_fusion.2 = f32[640,1280]{1,0:T(8,128)} fusion(bf16[1024,640]{0,1:T(8,128)(2,1)} %mul.117, pred[1024,1280]{0,1:T(32,128)(4,1)S(1)} %eq.120, f32[640,1280]{1,0:T(8,128)} %get-tuple-element.161, pred[]{:T(512)S(6)} %compare.3), kind=kOutput, calls=%fused_computation.1.clone.1 | convolution fusion | flops 1679360000 | bytes 9175041 | tf_op jit(solution)/shard_map/while/body/eval_jaxpr/dot_general | solution.py:59
  33.2 0.8 convolution_reduce_fusion.5
  34.0 0.4 iota_compare_fusion.5
  34.4 0.4 eq.121
  34.8 0.5 convolution_reduce_fusion.4
  35.3 0.0 copy-done.1
  35.4 1.5 constant_dynamic-slice_fusion.7
  36.9 0.5 broadcast_select_fusion.2
  37.4 1.2 mul.117
  38.7 0.9 iota_compare_fusion.4
  39.6 0.7 eq.120
  40.3 6.0 %convolution_add_fusion.2 = f32[640,1280]{1,0:T(8,128)} fusion(bf16[1024,640]{0,1:T(8,128)(2,1)} %mul.117, pred[1024,1280]{0,1:T(32,128)(4,1)S(1)} %eq.120, f32[640,1280]{1,0:T(8,128)} %get-tuple-element.161, pred[]{:T(512)S(6)} %compare.3), kind=kOutput, calls=%fused_computation.1.clone.1 | convolution fusion | flops 1679360000 | bytes 9175041 | tf_op jit(solution)/shard_map/while/body/eval_jaxpr/dot_general | solution.py:59
  46.4 0.8 convolution_reduce_fusion.5
  47.2 0.4 iota_compare_fusion.5
  47.6 0.4 eq.121
  48.0 0.5 convolution_reduce_fusion.4
  48.5 1.5 constant_dynamic-slice_fusion.7
  50.1 0.5 broadcast_select_fusion.2
  50.6 1.2 mul.117
  51.8 0.9 iota_compare_fusion.4
  52.8 0.7 eq.120
  53.5 6.0 %convolution_add_fusion.2 = f32[640,1280]{1,0:T(8,128)} fusion(bf16[1024,640]{0,1:T(8,128)(2,1)} %mul.117, pred[1024,1280]{0,1:T(32,128)(4,1)S(1)} %eq.120, f32[640,1280]{1,0:T(8,128)} %get-tuple-element.161, pred[]{:T(512)S(6)} %compare.3), kind=kOutput, calls=%fused_computation.1.clone.1 | convolution fusion | flops 1679360000 | bytes 9175041 | tf_op jit(solution)/shard_map/while/body/eval_jaxpr/dot_general | solution.py:59
  59.6 0.8 convolution_reduce_fusion.5
  60.4 0.4 iota_compare_fusion.5
  60.8 0.4 eq.121
  61.2 0.5 convolution_reduce_fusion.4
  61.7 1.5 constant_dynamic-slice_fusion.7
  63.3 0.5 broadcast_select_fusion.2
  63.8 1.2 mul.117
  65.0 0.9 iota_compare_fusion.4
  66.0 0.7 eq.120
  66.7 6.0 %convolution_add_fusion.2 = f32[640,1280]{1,0:T(8,128)} fusion(bf16[1024,640]{0,1:T(8,128)(2,1)} %mul.117, pred[1024,1280]{0,1:T(32,128)(4,1)S(1)} %eq.120, f32[640,1280]{1,0:T(8,128)} %get-tuple-element.161, pred[]{:T(512)S(6)} %compare.3), kind=kOutput, calls=%fused_computation.1.clone.1 | convolution fusion | flops 1679360000 | bytes 9175041 | tf_op jit(solution)/shard_map/while/body/eval_jaxpr/dot_general | solution.py:59
  72.8 0.8 convolution_reduce_fusion.5
  73.6 0.4 iota_compare_fusion.5
  74.0 0.4 eq.121
  74.4 0.5 convolution_reduce_fusion.4
  74.9 0.0 copy-start.2
  74.9 0.0 reduce-scatter.2.cloned.1.call-update
  74.9 0.0 all-gather.3.cloned.1.call-start
  75.0 36.3 %all-reduce = (f32[1280]{0:T(1024)S(1)}, f32[]{:T(128)}, f32[640]{0:T(1024)S(1)}) all-reduce(f32[1280]{0:T(1024)S(1)} %get-tuple-element.46, f32[]{:T(128)} %get-tuple-element.102, f32[640]{0:T(1024)S(1)} %get-tuple-element.45), channel_id=1, replica_groups=mesh['seq'=8,'row'=8,'col'=4] {'seq'}, use_global_device_ids=true, to_apply=%region_6.7 | all-reduce | flops 1921 | bytes 15368 | tf_op jit(solution)/shard_map/psum | solution.py:110
  111.3 0.7 divide_add_fusion.1
  112.1 0.7 divide_add_fusion
  112.7 51.2 %reduce-scatter.2.cloned.1.call-done = f32[80,1280]{1,0:T(8,128)} async-done(((f32[640,1280]{1,0:T(8,128)}), f32[80,1280]{1,0:T(8,128)}) %reduce-scatter.2.cloned.1.call-update) | async-done | bytes 409616 | tf_op jit(solution)/shard_map/reduce_scatter | solution.py:113
  163.9 1.8 multiply_subtract_fusion
  165.8 5.5 %all-gather = f32[320,128]{1,0:T(8,128)S(1)} all-gather(f32[80,128]{1,0:T(8,128)S(1)} %slice_select_fusion), channel_id=2, replica_groups=mesh['seq'=8,'row'=8,'col'=4] {'col'}, dimensions={0}, use_global_device_ids=true | all-gather | bytes 204800 | tf_op jit(solution)/shard_map/all_gather | solution.py:14
  171.3 0.6 reduce_sum.19
  171.9 0.0 all-gather.3.cloned.1.call-update
  172.0 0.1 copy.13
  172.1 1.0 fusion.6
  173.0 118.7 %all-gather.3.cloned.1.call-done = f32[5120,128]{1,0:T(8,128)} async-done(((f32[80,128]{1,0:T(8,128)}), f32[5120,128]{1,0:T(8,128)}) %all-gather.3.cloned.1.call-update) | async-done | bytes 2621456 | tf_op jit(solution)/shard_map/all_gather | solution.py:121
  291.8 2.6 fusion.3
  (50 shorter events, 0.5 us)
Async XLA Ops:
  6.5 157.4 %reduce-scatter.2.cloned.1.call-start = ((), (), s32[]{:S(2)}) async-start(), calls=%async_computation.1 | async-start | bytes 3686400 | tf_op jit(solution)/shard_map/reduce_scatter | solution.py:113
  20.1 2.3 copy-start.3
  23.1 3.3 %copy-start = (s32[4,1024,64]{1,2,0:T(8,128)}, s32[4,1024,64]{1,2,0:T(8,128)S(1)}, u32[]{:S(2)}) copy-start(s32[4,1024,64]{1,2,0:T(8,128)S(1)} %get-tuple-element.175) | copy-start | bytes 3145732 | tf_op jit(solution)/shard_map/while
  33.2 2.1 copy-start.1
  35.3 3.3 %copy-start = (s32[4,1024,64]{1,2,0:T(8,128)}, s32[4,1024,64]{1,2,0:T(8,128)S(1)}, u32[]{:S(2)}) copy-start(s32[4,1024,64]{1,2,0:T(8,128)S(1)} %get-tuple-element.175) | copy-start | bytes 3145732 | tf_op jit(solution)/shard_map/while
  46.4 2.1 copy-start.1
  48.5 3.3 %copy-start = (s32[4,1024,64]{1,2,0:T(8,128)}, s32[4,1024,64]{1,2,0:T(8,128)S(1)}, u32[]{:S(2)}) copy-start(s32[4,1024,64]{1,2,0:T(8,128)S(1)} %get-tuple-element.175) | copy-start | bytes 3145732 | tf_op jit(solution)/shard_map/while
  59.6 2.1 copy-start.1
  61.7 3.3 %copy-start = (s32[4,1024,64]{1,2,0:T(8,128)}, s32[4,1024,64]{1,2,0:T(8,128)S(1)}, u32[]{:S(2)}) copy-start(s32[4,1024,64]{1,2,0:T(8,128)S(1)} %get-tuple-element.175) | copy-start | bytes 3145732 | tf_op jit(solution)/shard_map/while
  72.8 2.1 copy-start.1
  74.9 97.1 %copy-start.2 = (f32[128,128]{1,0:T(8,128)S(1)}, f32[128,128]{1,0:T(8,128)}, u32[]{:S(2)}) copy-start(f32[128,128]{1,0:T(8,128)} %param.7) | copy-start | bytes 196612
  74.9 216.9 %all-gather.3.cloned.1.call-start = ((), (), s32[]{:S(2)}) async-start(), calls=%async_computation.2 | async-start | bytes 2662400 | tf_op jit(solution)/shard_map/all_gather | solution.py:121
Sparse Core Ops, SparseCore 0:
  75.0 88.8 reduce-scatter.1
  172.1 119.6 all-gather.2
